TPU v7x, 256 devices: a whole 4x4x8 slice. The times are simulated.
256 devices in a mesh: outer: 8 (over x, core), inner: 32 (over z, y).
Axes of the slice: x: 4, y: 4, z: 8, core: 2. Of those that a mesh axis runs over, the one named last changes fastest.
Arguments:
- query_rows: bfloat16 [98304, 2048], P(('outer', 'inner')), may hold values from -1.5 to 1.5
- key_rows: bfloat16 [98304, 2048], P(('outer', 'inner')), may hold values from -6 to 6
- value_rows: bfloat16 [98304, 2048], P(('outer', 'inner')), may hold values from -6 to 6
- grad_output: bfloat16 [98304, 2048], P(('outer', 'inner')), may hold values from -0.59765625 to 0.59765625
Outputs:
- grad_query: bfloat16 [98304, 2048], P(('outer', 'inner'))
- grad_key: bfloat16 [98304, 2048], P(('outer', 'inner'))
- grad_value: bfloat16 [98304, 2048], P(('outer', 'inner'))
All inputs are finite; a program needn't handle non-finite values.
Results may differ from a plain program's by a relative error of at most 0.0058.
Values may be sent and summed in bfloat16 or wider, within the bound.
A program may use at most 64 MiB of HBM per device.

v0:
```python
import jax
import jax.numpy as jnp
from jax import lax
from jax.sharding import PartitionSpec as P

HEADS = 16
HEAD = 128


def across_blocks(totals):
    every = lax.all_gather(totals[None], "outer", axis=0, tiled=True)
    place = lax.axis_index("outer")
    order = lax.iota(jnp.int32, every.shape[0])
    earlier = (order < place).astype(jnp.float32)[:, None, None]
    later = (order > place).astype(jnp.float32)[:, None, None]
    return (jnp.sum(every[:, 0] * earlier, axis=0), jnp.sum(every[:, 1] * later, axis=0))


def local(query_rows, key_rows, value_rows, grad_output):
    length = query_rows.shape[0]
    width = query_rows.shape[1]
    query = query_rows.reshape(length, HEADS, HEAD)
    key = key_rows.reshape(length, HEADS, HEAD)
    value = value_rows.reshape(length, HEADS, HEAD)
    grad = grad_output.reshape(length, HEADS, HEAD)
    offset = (lax.axis_index("outer") * lax.axis_size("inner") + lax.axis_index("inner")) * length
    positions = (offset + lax.iota(jnp.int32, length)).astype(jnp.float32)
    scales = 1.0 / jnp.sqrt(positions + 1.0)
    own_prefix = jnp.einsum("shd,she->hde", key, value, preferred_element_type=jnp.float32)
    scaled_grad = (grad.astype(jnp.float32) * scales[:, None, None]).astype(jnp.bfloat16)
    own_suffix = jnp.einsum("thd,the->hde", query, scaled_grad, preferred_element_type=jnp.float32)
    flat_prefix = own_prefix.reshape(HEADS * HEAD, HEAD)
    flat_suffix = own_suffix.reshape(HEADS * HEAD, HEAD)
    stacked = jnp.stack([flat_prefix, flat_suffix])[None]
    received = lax.all_to_all(stacked, "inner", split_axis=2, concat_axis=0, tiled=True)
    running = jnp.cumsum(received, axis=0)
    totals = running[-1]
    outer_before, outer_after = across_blocks(totals)
    before_part = running[:, 0] - received[:, 0] + outer_before[None]
    after_part = totals[1][None] - running[:, 1] + outer_after[None]
    outgoing = jnp.stack([before_part, after_part], axis=1).astype(jnp.bfloat16)
    returned = lax.all_to_all(outgoing, "inner", split_axis=0, concat_axis=2, tiled=True)
    before = returned[0, 0]
    after = returned[0, 1]
    prefix_state = before.reshape(HEADS, HEAD, HEAD)
    suffix_state = after.reshape(HEADS, HEAD, HEAD)
    order = lax.iota(jnp.int32, length)
    causal = (order[None, :] <= order[:, None])[None]
    prod_out = jnp.einsum("the,she->hts", grad, value, preferred_element_type=jnp.float32)
    prod_in = jnp.einsum("thd,shd->hts", query, key, preferred_element_type=jnp.float32)
    weight_out = (jnp.where(causal, prod_out, 0.0) * scales[None, :, None]).astype(jnp.bfloat16)
    weight_in = (jnp.where(causal, prod_in, 0.0) * scales[None, :, None]).astype(jnp.bfloat16)
    grad_q = scales[:, None, None] * jnp.einsum(
        "the,hde->thd", grad, prefix_state, preferred_element_type=jnp.float32
    )
    grad_q = grad_q + jnp.einsum(
        "hts,shd->thd", weight_out, key, preferred_element_type=jnp.float32
    )
    grad_k = jnp.einsum("she,hde->shd", value, suffix_state, preferred_element_type=jnp.float32)
    grad_k = grad_k + jnp.einsum(
        "hts,thd->shd", weight_out, query, preferred_element_type=jnp.float32
    )
    grad_v = jnp.einsum("shd,hde->she", key, suffix_state, preferred_element_type=jnp.float32)
    grad_v = grad_v + jnp.einsum(
        "hts,the->she", weight_in, grad, preferred_element_type=jnp.float32
    )
    return (
        grad_q.reshape(length, width).astype(jnp.bfloat16),
        grad_k.reshape(length, width).astype(jnp.bfloat16),
        grad_v.reshape(length, width).astype(jnp.bfloat16),
    )


def solution(mesh):
    placed = (
        P(("outer", "inner"), None),
        P(("outer", "inner"), None),
        P(("outer", "inner"), None),
        P(("outer", "inner"), None),
    )
    return jax.shard_map(
        local,
        mesh=mesh,
        in_specs=placed,
        out_specs=(
            P(("outer", "inner"), None),
            P(("outer", "inner"), None),
            P(("outer", "inner"), None),
        ),
        check_vma=False,
    )
```

profile of v0, /device:TPU:1, one launch (start us, length us, event | category | flops | bytes accessed | tf_op | source)
XLA Modules:
  0.0 152.0 jit_solution(15195193522482980512)
XLA Ops:
  0.6 0.0 copy-start
  0.7 0.0 copy-start.4
  0.7 2.7 %fusion.22 = f32[16,128,128]{2,1,0:T(8,128)S(1)} fusion(bf16[384,2048]{1,0:T(8,128)(2,1)} %param.6, bf16[384,2048]{1,0:T(8,128)(2,1)} %param.5), kind=kOutput, calls=%fused_computation.28 | convolution fusion | flops 201326592 | bytes 4194304 | tf_op jit(solution)/shard_map/shd,she->hde/dot_general | solution.py:29
  3.4 0.0 copy-done
  3.4 0.0 copy-done.4
  3.5 0.9 fusion.9
  4.4 2.9 %maximum_bitcast_fusion = f32[1,2,2048,128]{3,1,0,2:T(2,128)} fusion(f32[1,2048,128]{2,0,1:T(1,128)S(1)} %bitcast.158, f32[1,2048,128]{2,0,1:T(1,128)S(1)} %bitcast.155), kind=kLoop, calls=%fused_computation.14 | loop fusion | flops 524288 | bytes 4194304 | tf_op jit(solution)/shard_map/broadcast_in_dim | solution.py:34
  7.3 12.2 %all-to-all-start = ((f32[1,2,2048,128]{3,1,0,2:T(2,128)}), f32[1,2,2048,128]{3,1,0,2:T(2,128)}, u32[]{:S(2)}, u32[]{:S(2)}) async-start(f32[1,2,2048,128]{3,1,0,2:T(2,128)} %maximum_bitcast_fusion), calls=%async_computation | async-start | bytes 4194304 | tf_op jit(solution)/shard_map/all_to_all | solution.py:35
  19.5 48.4 %all-to-all-done = f32[1,2,2048,128]{3,1,0,2:T(2,128)} async-done(((f32[1,2,2048,128]{3,1,0,2:T(2,128)}), f32[1,2,2048,128]{3,1,0,2:T(2,128)}, u32[]{:S(2)}, u32[]{:S(2)}) %all-to-all-start) | async-done | bytes 2097184 | tf_op jit(solution)/shard_map/all_to_all | solution.py:35
  67.9 1.7 %fusion.56 = f32[32,2,64,128]{3,2,1,0:T(8,128)S(1)} fusion(f32[1,2,32,64,128]{4,1,3,2,0:T(2,128)} %bitcast.6), kind=kOutput, calls=%fused_computation.69 | output fusion | flops 16252928 | bytes 4194304 | tf_op jit(solution)/shard_map/jit(cumsum)/reduce_window_sum | solution.py:36
  69.7 1.9 %copy.131 = f32[1,2,32,64,128]{4,3,1,2,0:T(8,128)S(1)} copy(f32[1,2,32,64,128]{4,1,3,2,0:T(2,128)} %bitcast.6) | data formatting | bytes 4194304 | tf_op jit(solution)/shard_map/all_to_all | solution.py:35
  71.6 15.9 %all_gather.3 = f32[8,2,64,128]{3,2,1,0:T(8,128)S(1)} all-gather(f32[1,2,64,128]{3,2,1,0:T(8,128)S(1)} %slice.40), channel_id=1, replica_groups=mesh['outer'=8,'inner'=32] {'outer'}, dimensions={0}, use_global_device_ids=true | all-gather | bytes 589824 | tf_op jit(solution)/shard_map/all_gather | solution.py:11
  87.5 0.1 fusion.54
  87.6 0.4 fusion.41
  88.0 1.1 pad_maximum_fusion
  89.1 0.0 copy-start.2
  89.1 6.1 %all-to-all-start.1 = ((bf16[32,2,64,128]{3,2,1,0:T(8,128)(2,1)}), bf16[32,2,64,128]{3,2,1,0:T(8,128)(2,1)}, u32[]{:S(2)}, u32[]{:S(2)}) async-start(bf16[32,2,64,128]{3,2,1,0:T(8,128)(2,1)} %pad_maximum_fusion), calls=%async_computation.1 | async-start | bytes 2097152 | tf_op jit(solution)/shard_map/all_to_all | solution.py:42
  95.2 0.0 copy-done.2
  95.2 3.6 %multiply_convert_fusion.1 = bf16[16,384,384]{2,1,0:T(8,128)(2,1)} fusion(f32[384]{0:T(512)S(1)} %add_rsqrt_fusion, pred[384,384]{1,0:T(8,128)(4,1)S(1)} %iota_compare_fusion, bf16[384,2048]{1,0:T(8,128)(2,1)S(1)} %copy-done, bf16[384,2048]{1,0:T(8,128)(2,1)S(1)} %copy-done.2), kind=kOutput, calls=%fused_computation.1 | convolution fusion | flops 611057664 | bytes 8013312 | tf_op jit(solution)/shard_map/the,she->hts/dot_general | solution.py:49
  98.9 23.3 %all-to-all-done.1 = bf16[32,2,64,128]{3,2,1,0:T(8,128)(2,1)} async-done(((bf16[32,2,64,128]{3,2,1,0:T(8,128)(2,1)}), bf16[32,2,64,128]{3,2,1,0:T(8,128)(2,1)}, u32[]{:S(2)}, u32[]{:S(2)}) %all-to-all-start.1) | async-done | bytes 1048608 | tf_op jit(solution)/shard_map/all_to_all | solution.py:42
  122.2 0.0 copy-start.3
  122.2 1.4 copy.49
  123.6 0.0 slice-start
  123.6 0.9 fusion.57
  124.5 0.0 copy-done.3
  124.5 0.0 copy-start.1
  124.5 0.0 slice-start.1
  124.5 0.8 fusion.19
  125.3 1.1 copy-done.1
  126.5 0.0 copy-start.5
  126.5 2.5 %fusion.28 = f32[16,128,384]{2,1,0:T(8,128)} fusion(bf16[16,128,128]{2,1,0:T(8,128)(2,1)S(1)} %bitcast.152, bf16[384,2048]{1,0:T(8,128)(2,1)S(1)} %copy-done.1), kind=kOutput, calls=%fused_computation.33 | convolution fusion | flops 201326592 | bytes 5242880 | tf_op jit(solution)/shard_map/shd,hde->she/dot_general | solution.py:63
  128.9 0.0 slice-done
  128.9 0.0 slice-done.1
  128.9 0.0 copy-done.5
  128.9 2.4 %fusion.7 = bf16[384,16,128]{0,2,1:T(8,128)(2,1)} fusion(f32[16,128,384]{2,1,0:T(8,128)S(1)} %fusion.19, bf16[16,384,384]{2,1,0:T(8,128)(2,1)S(1)} %bitcast.148, bf16[384,2048]{1,0:T(8,128)(2,1)S(1)} %copy-done.5), kind=kOutput, calls=%fused_computation.10 | convolution fusion | flops 605552640 | bytes 11010048 | tf_op jit(solution)/shard_map/hts,thd->shd/dot_general | solution.py:60
  131.3 2.6 %copy.62 = bf16[384,2048]{1,0:T(8,128)(2,1)} copy(bf16[384,2048]{0,1:T(8,128)(2,1)} %bitcast.150) | data formatting | bytes 3145728
  133.9 1.8 %fusion.11 = f32[16,128,384]{2,1,0:T(8,128)S(1)} fusion(bf16[16,128,128]{2,1,0:T(8,128)(2,1)} %bitcast.156, bf16[384,2048]{1,0:T(8,128)(2,1)S(1)} %copy-done), kind=kOutput, calls=%fused_computation.18 | convolution fusion | flops 201326592 | bytes 5242880 | tf_op jit(solution)/shard_map/the,hde->thd/dot_general | solution.py:53
  135.7 5.1 %fusion.8 = bf16[384,16,128]{0,2,1:T(8,128)(2,1)} fusion(f32[16,128,384]{2,1,0:T(8,128)S(1)} %fusion.11, bf16[16,384,384]{2,1,0:T(8,128)(2,1)} %multiply_convert_fusion.1, f32[384]{0:T(512)S(1)} %add_rsqrt_fusion, bf16[384,2048]{1,0:T(8,128)(2,1)S(1)} %copy-done.1), kind=kOutput, calls=%fused_computation.12 | convolution fusion | flops 606339072 | bytes 11011584 | tf_op jit(solution)/shard_map/hts,shd->thd/dot_general | solution.py:56
  140.8 2.6 %copy.61 = bf16[384,2048]{1,0:T(8,128)(2,1)} copy(bf16[384,2048]{0,1:T(8,128)(2,1)} %bitcast.149) | data formatting | bytes 3145728
  143.4 6.1 %fusion.6 = bf16[384,16,128]{0,2,1:T(8,128)(2,1)} fusion(f32[16,128,384]{2,1,0:T(8,128)} %fusion.28, f32[384]{0:T(512)S(1)} %add_rsqrt_fusion, pred[384,384]{1,0:T(8,128)(4,1)S(1)} %iota_compare_fusion, bf16[384,2048]{1,0:T(8,128)(2,1)S(1)} %copy-done, bf16[384,2048]{1,0:T(8,128)(2,1)} %param.4, bf16[384,2048]{1,0:T(8,128)(2,1)S(1)} %copy-done.1), kind=kOutput, calls=%fused_computation.8 | convolution fusion | flops 1216610304 | bytes 9586176 | tf_op jit(solution)/shard_map/hts,the->she/dot_general | solution.py:64
  149.4 2.6 %copy.63 = bf16[384,2048]{1,0:T(8,128)(2,1)} copy(bf16[384,2048]{0,1:T(8,128)(2,1)} %bitcast.157) | data formatting | bytes 3145728
  (6 shorter events, 0.1 us)
Async XLA Ops:
  0.6 2.8 %copy-start = (bf16[384,2048]{1,0:T(8,128)(2,1)S(1)}, bf16[384,2048]{1,0:T(8,128)(2,1)}, u32[]{:S(2)}) copy-start(bf16[384,2048]{1,0:T(8,128)(2,1)} %param.7) | copy-start | bytes 4718596
  0.7 2.8 %copy-start.4 = (bf16[384,2048]{1,0:T(8,128)(2,1)S(1)}, bf16[384,2048]{1,0:T(8,128)(2,1)}, u32[]{:S(2)}) copy-start(bf16[384,2048]{1,0:T(8,128)(2,1)} %param.4) | copy-start | bytes 4718596
  7.3 60.6 %all-to-all-start = ((f32[1,2,2048,128]{3,1,0,2:T(2,128)}), f32[1,2,2048,128]{3,1,0,2:T(2,128)}, u32[]{:S(2)}, u32[]{:S(2)}) async-start(f32[1,2,2048,128]{3,1,0,2:T(2,128)} %maximum_bitcast_fusion), calls=%async_computation | async-start | bytes 4194304 | tf_op jit(solution)/shard_map/all_to_all | solution.py:35
  89.1 6.2 %copy-start.2 = (bf16[384,2048]{1,0:T(8,128)(2,1)S(1)}, bf16[384,2048]{1,0:T(8,128)(2,1)}, u32[]{:S(2)}) copy-start(bf16[384,2048]{1,0:T(8,128)(2,1)} %param.6) | copy-start | bytes 4718596
  89.1 33.1 %all-to-all-start.1 = ((bf16[32,2,64,128]{3,2,1,0:T(8,128)(2,1)}), bf16[32,2,64,128]{3,2,1,0:T(8,128)(2,1)}, u32[]{:S(2)}, u32[]{:S(2)}) async-start(bf16[32,2,64,128]{3,2,1,0:T(8,128)(2,1)} %pad_maximum_fusion), calls=%async_computation.1 | async-start | bytes 2097152 | tf_op jit(solution)/shard_map/all_to_all | solution.py:42
  122.2 2.3 %copy-start.3 = (bf16[384,2048]{1,0:T(8,128)(2,1)S(1)}, bf16[384,2048]{1,0:T(8,128)(2,1)}, u32[]{:S(2)}) copy-start(bf16[384,2048]{1,0:T(8,128)(2,1)} %param.6) | copy-start | bytes 4718596
  123.6 5.3 %slice-start = ((s8[4718592]{0:T(1024)(128)(4,1)}), s8[4194304]{0:T(1024)(128)(4,1)S(1)}, s32[]{:S(2)}) async-start(s8[4718592]{0:T(1024)(128)(4,1)} %bitcast.147), calls=%async_computation.2 | async-start | bytes 8388608
  124.5 1.9 %copy-start.1 = (bf16[384,2048]{1,0:T(8,128)(2,1)S(1)}, bf16[384,2048]{1,0:T(8,128)(2,1)}, u32[]{:S(2)}) copy-start(bf16[384,2048]{1,0:T(8,128)(2,1)} %param.5) | copy-start | bytes 4718596
  124.5 4.4 %slice-start.1 = ((s8[4718592]{0:T(1024)(128)(4,1)}), s8[524288]{0:T(1024)(128)(4,1)S(1)}, s32[]{:S(2)}) async-start(s8[4718592]{0:T(1024)(128)(4,1)} %bitcast.147), calls=%async_computation.3 | async-start | bytes 1048576
  126.5 2.5 %copy-start.5 = (bf16[384,2048]{1,0:T(8,128)(2,1)S(1)}, bf16[384,2048]{1,0:T(8,128)(2,1)}, u32[]{:S(2)}) copy-start(bf16[384,2048]{1,0:T(8,128)(2,1)} %param.4) | copy-start | bytes 4718596
where the time goes:
time: 153 us; the launch traced here: 152 us
  waiting for transfers between devices  71.8 us (47%)
  matrix products  25.9 us (17%)
  starting transfers between devices  18.3 us (12%)
  blocking collectives  15.9 us (10%)
  local copies, waits for them, and re-layouts  13.1 us (9%)
  other arithmetic  6.25 us (4%)
    all_to_all x1, waiting for transfers between devices, local(): lax.all_to_all(stacked, 'inner', split_axis=2, concat_axis=0, tiled=True)  48.4 us
    all_to_all x1, waiting for transfers between devices, local(): lax.all_to_all(outgoing, 'inner', split_axis=0, concat_axis=2, tiled=True)  23.3 us
    all_gather x1, blocking collectives, across_blocks(): every = lax.all_gather(totals[None], 'outer', axis=0, tiled=True)  15.9 us
    all_to_all x1, starting transfers between devices, local(): lax.all_to_all(stacked, 'inner', split_axis=2, concat_axis=0, tiled=True)  12.2 us
    unnamed x19, local copies, waits for them, and re-layouts  8.93 us
    all_to_all x1, starting transfers between devices, local(): lax.all_to_all(outgoing, 'inner', split_axis=0, concat_axis=2, tiled=True)  6.1 us
    dot_general x1, matrix products, local(): jnp.einsum('hts,the->she', weight_in, grad, preferred_element_type=jnp.fl...  6.06 us
    dot_general x1, matrix products, local(): jnp.einsum('hts,shd->thd', weight_out, key, preferred_element_type=jnp.fl...  5.07 us
  transfers between devices with their start and end apart: 2, of which 2 were waited for; matrix products, arithmetic and copies ran while one was open for 2% of the time, Pallas kernels for 0%

commit v1 on v0

v1 whole, which is shorter than its diff:
```python
import functools

import jax
import jax.numpy as jnp
from jax import lax
from jax.experimental import pallas as pl
from jax.experimental.pallas import tpu as pltpu
from jax.sharding import PartitionSpec as P

MESH = pl.DeviceIdType.MESH
HEADS = 16
HEAD = 128
NY = 4
CHUNKS = 4
F32 = jnp.float32
BF16 = jnp.bfloat16

NN = (((1,), (0,)), ((), ()))
NT = (((1,), (1,)), ((), ()))
TN = (((0,), (0,)), ((), ()))


def dot(a, b, dims):
    return lax.dot_general(a, b, dims, preferred_element_type=F32)


def far_first(count):
    return sorted(range(1, count), key=lambda step: -min(step, count - step))


def schedule():
    order = []
    for c in range(CHUNKS):
        order.append(("S", c))
    order.append(("I", 0, 6))
    order.append(("R", 0))
    order.append(("I", 6, 8))
    order.append(("R", 1))
    order.append(("I", 8, 10))
    order.append(("R", 2))
    order.append(("T", 0))
    order.append(("I", 10, 12))
    order.append(("R", 3))
    order.append(("T", 1))
    order.append(("Z", 0))
    order.append(("I", 12, 14))
    order.append(("T", 2))
    order.append(("Z", 1))
    order.append(("I", 14, 16))
    order.append(("T", 3))
    order.append(("P", 0))
    order.append(("Z", 2))
    order.append(("P", 1))
    order.append(("Z", 3))
    order.append(("P", 2))
    order.append(("F", 0))
    order.append(("P", 3))
    order.append(("F", 1))
    order.append(("F", 2))
    order.append(("F", 3))
    return order


def kernel(
    no, nz,
    q_hbm, k_hbm, v_hbm, g_hbm,
    oq_hbm, ok_hbm, ov_hbm,
    q, k, v, g, sg, pq, pk, pv, oq, ok, ov,
    ysend, yrecv, zsend, zrecv, tsend, trecv, bsend, brecv, psend, precv,
    in_sem, out_sem, send_sem, recv_sem,
):
    length = q.shape[0]
    per = HEADS // CHUNKS
    width = per * HEAD
    sub = HEAD // nz
    o = lax.axis_index("outer")
    i = lax.axis_index("inner")
    z = i // NY
    y = i % NY

    ypeers = [lax.rem(y + d, NY) for d in far_first(NY)]
    zpeers = [lax.rem(z + d, nz) for d in far_first(nz)]
    opeers = [lax.rem(o + d, no) for d in far_first(no)]

    def loads(c):
        cols = pl.ds(c * width, width)
        return [
            pltpu.make_async_copy(src.at[:, cols], dst.at[:, cols], in_sem.at[c, j])
            for j, (src, dst) in enumerate(((k_hbm, k), (v_hbm, v), (g_hbm, g), (q_hbm, q)))
        ]

    for c in range(CHUNKS):
        for copy in loads(c):
            copy.start()

    barrier = pltpu.get_barrier_semaphore()
    everyone = (
        [(o, z * NY + p) for p in ypeers]
        + [(o, p * NY + y) for p in zpeers]
        + [(p, i) for p in opeers]
    )
    for peer in everyone:
        pl.semaphore_signal(barrier, inc=1, device_id=peer, device_id_type=MESH)

    offset = (o * (nz * NY) + i) * length
    rows = lax.broadcasted_iota(jnp.int32, (length, HEAD), 0) + offset
    scales = lax.rsqrt(rows.astype(F32) + 1.0)

    def send(src, dst, stage, c, peer):
        pltpu.make_async_remote_copy(
            src_ref=src, dst_ref=dst, send_sem=send_sem.at[stage], recv_sem=recv_sem.at[stage, c],
            device_id=peer, device_id_type=MESH,
        ).start()

    def arrived(ref, stage, c):
        pltpu.make_async_copy(ref, ref, recv_sem.at[stage, c]).wait()

    def states(c):
        for copy in loads(c):
            copy.wait()
        for j in range(per):
            cols = pl.ds((c * per + j) * HEAD, HEAD)
            ysend[c * NY + j, 0] = dot(k[:, cols], v[:, cols], TN).astype(BF16)
            scaled = (g[:, cols].astype(F32) * scales).astype(BF16)
            sg[:, cols] = scaled
            ysend[c * NY + j, 1] = dot(q[:, cols], scaled, TN).astype(BF16)
        if c == 0:
            pl.semaphore_wait(barrier, len(everyone))
        for p in ypeers:
            send(ysend.at[c * NY + p], yrecv.at[c, y], 0, c, (o, z * NY + p))
        yrecv[c, y] = ysend[c * NY + y]

    def group_sums(c):
        arrived(yrecv.at[c, pl.ds(0, NY - 1)], 0, c)
        total = yrecv[c, 0].astype(F32)
        for p in range(1, NY):
            total = total + yrecv[c, p].astype(F32)
        total = total.astype(BF16)
        for p in range(nz):
            zsend[c * nz + p] = total[:, p * sub:(p + 1) * sub, :]
        for p in zpeers:
            send(zsend.at[c * nz + p], zrecv.at[c, z], 1, c, (o, p * NY + y))
        zrecv[c, z] = zsend[c * nz + z]

    def outer_totals(c):
        arrived(zrecv.at[c, pl.ds(0, nz - 1)], 1, c)
        tsend[c] = jnp.sum(zrecv[c].astype(F32), axis=0)
        for p in opeers:
            kind = jnp.where(p > o, 0, 1)
            send(tsend.at[c, kind], trecv.at[c, o], 2, c, (p, i))
        trecv[c, o] = jnp.zeros((sub, HEAD), F32)

    def offsets(c):
        arrived(trecv.at[c, pl.ds(0, no - 1)], 2, c)
        before = jnp.zeros((sub, HEAD), F32)
        after = jnp.zeros((sub, HEAD), F32)
        for p in range(no):
            part = trecv[c, p]
            before = before + jnp.where(p < o, part, 0.0)
            after = after + jnp.where(p > o, part, 0.0)
        for p in range(nz):
            bsend[c * nz + p, 0] = before.astype(BF16)
            before = before + zrecv[c, p, 0].astype(F32)
        for p in reversed(range(nz)):
            bsend[c * nz + p, 1] = after.astype(BF16)
            after = after + zrecv[c, p, 1].astype(F32)
        for p in zpeers:
            send(bsend.at[c * nz + p], brecv.at[c, z], 3, c, (o, p * NY + y))
        brecv[c, z] = bsend[c * nz + z]

    def block_states(c):
        arrived(brecv.at[c, pl.ds(0, nz - 1)], 3, c)
        for p in range(nz):
            part = pl.ds(p * sub, sub)
            before = brecv[c, p, 0].astype(F32)
            for r in range(NY):
                psend[c * NY + r, 0, part] = before.astype(BF16)
                before = before + yrecv[c, r, 0, part].astype(F32)
            after = brecv[c, p, 1].astype(F32)
            for r in reversed(range(NY)):
                psend[c * NY + r, 1, part] = after.astype(BF16)
                after = after + yrecv[c, r, 1, part].astype(F32)
        for p in ypeers:
            send(psend.at[c * NY + p], precv.at[c, y], 4, c, (o, z * NY + p))
        precv[c, y] = psend[c * NY + y]

    def stores(c):
        cols = pl.ds(c * width, width)
        return [
            pltpu.make_async_copy(src.at[:, cols], dst.at[:, cols], out_sem.at[c, j])
            for j, (src, dst) in enumerate(((oq, oq_hbm), (ok, ok_hbm), (ov, ov_hbm)))
        ]

    def finish(c):
        arrived(precv.at[c, pl.ds(0, NY - 1)], 4, c)
        for j in range(per):
            cols = pl.ds((c * per + j) * HEAD, HEAD)
            prefix = precv[c, j, 0]
            suffix = precv[c, j, 1]
            oq[:, cols] = (pq[:, cols] + dot(sg[:, cols], prefix, NT)).astype(BF16)
            ok[:, cols] = (pk[:, cols] + dot(v[:, cols], suffix, NT)).astype(BF16)
            ov[:, cols] = (pv[:, cols] + dot(k[:, cols], suffix, NN)).astype(BF16)
        for copy in stores(c):
            copy.start()

    cut = length - HEAD

    def inside(head, carry):
        cols = pl.ds(pl.multiple_of(head * HEAD, HEAD), HEAD)
        kh, vh, qh, sh = k[:, cols], v[:, cols], q[:, cols], sg[:, cols]
        first = lax.broadcasted_iota(jnp.int32, (length, cut), 0)
        second = lax.broadcasted_iota(jnp.int32, (length, cut), 1)
        lower = second <= first
        upper = first <= second + HEAD
        row = lax.broadcasted_iota(jnp.int32, (HEAD, HEAD), 0)
        col = lax.broadcasted_iota(jnp.int32, (HEAD, HEAD), 1)

        def masked(a, b, mask):
            return jnp.where(mask, dot(a, b, NT), 0.0).astype(BF16)

        main = dot(masked(sh, vh[:cut], lower), kh[:cut], NN)
        rest = dot(masked(sh[cut:], vh[cut:], col <= row), kh[cut:], NN)
        pq[:cut, cols] = main[:cut]
        pq[cut:, cols] = main[cut:] + rest
        main = dot(masked(vh, sh[HEAD:], upper), qh[HEAD:], NN)
        rest = dot(masked(vh[:HEAD], sh[:HEAD], row <= col), qh[:HEAD], NN)
        pk[:HEAD, cols] = main[:HEAD] + rest
        pk[HEAD:, cols] = main[HEAD:]
        main = dot(masked(kh, qh[HEAD:], upper), sh[HEAD:], NN)
        rest = dot(masked(kh[:HEAD], qh[:HEAD], row <= col), sh[:HEAD], NN)
        pv[:HEAD, cols] = main[:HEAD] + rest
        pv[HEAD:, cols] = main[HEAD:]
        return carry

    actions = {
        "S": states, "R": group_sums, "T": outer_totals, "Z": offsets, "P": block_states, "F": finish,
    }
    for step in schedule():
        if step[0] == "I":
            lax.fori_loop(step[1], step[2], inside, 0)
        else:
            actions[step[0]](step[1])

    for c in range(CHUNKS):
        for copy in stores(c):
            copy.wait()

    def sent(ref, stage):
        pltpu.make_async_copy(ref, ref, send_sem.at[stage]).wait()

    sent(ysend.at[pl.ds(0, CHUNKS * (NY - 1))], 0)
    sent(zsend.at[pl.ds(0, CHUNKS * (nz - 1))], 1)
    for c in range(CHUNKS):
        sent(trecv.at[c, pl.ds(0, no - 1)], 2)
    sent(bsend.at[pl.ds(0, CHUNKS * (nz - 1))], 3)
    sent(psend.at[pl.ds(0, CHUNKS * (NY - 1))], 4)


def solution(mesh):
    no = mesh.shape["outer"]
    nz = mesh.shape["inner"] // NY
    sub = HEAD // nz

    def local(query_rows, key_rows, value_rows, grad_output):
        shape = query_rows.shape
        out = jax.ShapeDtypeStruct(shape, BF16)
        anywhere = pl.BlockSpec(memory_space=pl.ANY)
        return pl.pallas_call(
            functools.partial(kernel, no, nz),
            name="linear_attention_grads",
            out_shape=(out, out, out),
            in_specs=[anywhere] * 4,
            out_specs=(anywhere,) * 3,
            scratch_shapes=(
                [pltpu.VMEM(shape, BF16)] * 5
                + [pltpu.VMEM(shape, F32)] * 3
                + [pltpu.VMEM(shape, BF16)] * 3
                + [
                    pltpu.VMEM((CHUNKS * NY, 2, HEAD, HEAD), BF16),
                    pltpu.VMEM((CHUNKS, NY, 2, HEAD, HEAD), BF16),
                    pltpu.VMEM((CHUNKS * nz, 2, sub, HEAD), BF16),
                    pltpu.VMEM((CHUNKS, nz, 2, sub, HEAD), BF16),
                    pltpu.VMEM((CHUNKS, 2, sub, HEAD), F32),
                    pltpu.VMEM((CHUNKS, no, sub, HEAD), F32),
                    pltpu.VMEM((CHUNKS * nz, 2, sub, HEAD), BF16),
                    pltpu.VMEM((CHUNKS, nz, 2, sub, HEAD), BF16),
                    pltpu.VMEM((CHUNKS * NY, 2, HEAD, HEAD), BF16),
                    pltpu.VMEM((CHUNKS, NY, 2, HEAD, HEAD), BF16),
                    pltpu.SemaphoreType.DMA((CHUNKS, 4)),
                    pltpu.SemaphoreType.DMA((CHUNKS, 3)),
                    pltpu.SemaphoreType.DMA((5,)),
                    pltpu.SemaphoreType.DMA((5, CHUNKS)),
                ]
            ),
            compiler_params=pltpu.CompilerParams(
                collective_id=0, has_side_effects=True, vmem_limit_bytes=48 << 20
            ),
        )(query_rows, key_rows, value_rows, grad_output)

    placed = P(("outer", "inner"), None)
    return jax.shard_map(
        local, mesh=mesh, in_specs=(placed,) * 4, out_specs=(placed,) * 3, check_vma=False
    )
```

time: 153 us -> 47.8 us (0.31)
  waiting for transfers between devices: 71.8 us -> 0 us
  Pallas kernels: 0 us -> 43.7 us
  matrix products: 25.9 us -> 0 us
  starting transfers between devices: 18.3 us -> 0 us
  blocking collectives: 15.9 us -> 0 us
  local copies, waits for them, and re-layouts: 13.1 us -> 3.43 us
  other arithmetic: 6.25 us -> 0 us
    all_to_all x2 -> x0, waiting for transfers between devices: 71.8 us -> none  [the longest x1 48.4 us: local(): lax.all_to_all(stacked, 'inner', split_axis=2, concat_axis=0, tiled=True)]
    pallas_call x0 -> x1, Pallas kernels: none -> 43.7 us  [local(): pl.pallas_call(functools.partial(kernel, no, nz), name='linear_attention_...]
    dot_general x9 -> x0, matrix products: 25.9 us -> none  [the longest x1 6.06 us: local(): jnp.einsum('hts,the->she', weight_in, grad, preferred_element_type=jnp.fl...]
    all_to_all x2 -> x0, starting transfers between devices: 18.3 us -> none  [the longest x1 12.2 us: local(): lax.all_to_all(stacked, 'inner', split_axis=2, concat_axis=0, tiled=True)]
    all_gather x1 -> x0, blocking collectives: 15.9 us -> none  [across_blocks(): every = lax.all_gather(totals[None], 'outer', axis=0, tiled=True)]
    unnamed x19 -> x3, local copies, waits for them, and re-layouts: 8.93 us -> 3.43 us
    all_to_all x2 -> x0, local copies, waits for them, and re-layouts: 3.28 us -> none  [the longest x1 1.86 us: local(): lax.all_to_all(stacked, 'inner', split_axis=2, concat_axis=0, tiled=True)]
    another operation x3 -> x0, other arithmetic: 3.16 us -> none  [the longest x1 1.74 us: local(): running = jnp.cumsum(received, axis=0)]
  transfers between devices with their start and end apart: 2 -> 0, of which waited for: 2 -> 0; matrix products, arithmetic and copies ran while one was open for 2% -> 0% of each run, Pallas kernels for 0% -> 0%
where the time goes in v1:
time: 47.8 us
  Pallas kernels  43.7 us (91%)
  local copies, waits for them, and re-layouts  3.43 us (7%)
  between operations  0.64 us (1%)
    pallas_call x1, Pallas kernels, local(): pl.pallas_call(functools.partial(kernel, no, nz), name='linear_attention_...  43.7 us
    unnamed x3, local copies, waits for them, and re-layouts  3.43 us

profile of v1, /device:TPU:1, one launch (start us, length us, event | category | flops | bytes accessed | tf_op | source)
XLA Modules:
  0.0 47.8 jit_solution(10305927449990022114)
XLA Ops:
  0.6 43.7 %linear_attention_grads.1 = (bf16[384,2048]{1,0:T(8,128)(2,1)S(1)}, bf16[384,2048]{1,0:T(8,128)(2,1)S(1)}, bf16[384,2048]{1,0:T(8,128)(2,1)S(1)}) custom-call(bf16[384,2048]{1,0:T(8,128)(2,1)} %q_hbm.1, bf16[384,2048]{1,0:T(8,128)(2,1)} %k_hbm.1, bf16[384,2048]{1,0:T(8,128)(2,1)} %v_hbm.1, bf16[384,2048]{1,0:T(8,128)(2,1)} %g_hbm.1), custom_call_target="tpu_custom_call" | custom-call | tf_op jit(solution)/shard_map/linear_attention_grads/pallas_call | solution.py:268
  44.3 1.1 %copy.10 = bf16[384,2048]{1,0:T(8,128)(2,1)} copy(bf16[384,2048]{1,0:T(8,128)(2,1)S(1)} %get-tuple-element.6) | data formatting | bytes 3145728
  45.5 1.1 %copy.11 = bf16[384,2048]{1,0:T(8,128)(2,1)} copy(bf16[384,2048]{1,0:T(8,128)(2,1)S(1)} %get-tuple-element.7) | data formatting | bytes 3145728
  46.6 1.1 %copy.12 = bf16[384,2048]{1,0:T(8,128)(2,1)} copy(bf16[384,2048]{1,0:T(8,128)(2,1)S(1)} %get-tuple-element.8) | data formatting | bytes 3145728

commit v2 on v1

v2 whole, which is shorter than its diff:
```python
import functools

import jax
import jax.numpy as jnp
from jax import lax
from jax.experimental import pallas as pl
from jax.experimental.pallas import tpu as pltpu
from jax.sharding import PartitionSpec as P

MESH = pl.DeviceIdType.MESH
HEADS = 16
HEAD = 128
NY = 4
PARTS = (4, 4, 4, 4)
CHUNKS = len(PARTS)
ORDER = (
    "S0 S1 S2 S3 "
    "I6 R0 I2 R1 "
    "I2 R2 T0 I2 "
    "R3 T1 Z0 I2 "
    "T2 Z1 I2 L0 "
    "T3 P0 Z2 P1 "
    "Z3 P2 P3 F0 "
    "F1 F2 "
)
LIMIT = 90 << 19
START = [sum(PARTS[:c]) for c in range(CHUNKS)]
F32 = jnp.float32
BF16 = jnp.bfloat16

NN = (((1,), (0,)), ((), ()))
NT = (((1,), (1,)), ((), ()))
TN = (((0,), (0,)), ((), ()))


def dot(a, b, dims):
    return lax.dot_general(a, b, dims, preferred_element_type=F32)


def far_first(count):
    return sorted(range(1, count), key=lambda step: -min(step, count - step))


def schedule():
    order = []
    inner = 0
    for step in ORDER.split():
        if step[0] == "I":
            count = int(step[1:])
            order.append(("I", inner, inner + count))
            inner += count
        else:
            order.append((step[0], int(step[1:])))
    return order


def kernel(no, nz, *refs):
    refs = iter(refs)

    def take(count):
        return [next(refs) for _ in range(count)]

    q_hbm, k_hbm, v_hbm, g_hbm = take(4)
    oq, ok, ov, lq, lk, lv, ls, lw, lx, last_states = take(10)
    q, k, v, g, sg, pq, pk, pv = take(8)
    ysend, yrecv, zsend, zrecv, tsend, trecv, bsend, brecv, psend = (take(CHUNKS) for _ in range(9))
    precv = take(CHUNKS - 1)
    in_sem, send_sem, recv_sem = take(3)
    precv.append(last_states)
    length = q.shape[0]
    o = lax.axis_index("outer")
    i = lax.axis_index("inner")
    z = i // NY
    y = i % NY

    ypeers = [lax.rem(y + d, NY) for d in far_first(NY)]
    zpeers = [lax.rem(z + d, nz) for d in far_first(nz)]
    opeers = [lax.rem(o + d, no) for d in far_first(no)]

    def loads(c):
        cols = pl.ds(START[c] * HEAD, PARTS[c] * HEAD)
        return [
            pltpu.make_async_copy(src.at[:, cols], dst.at[:, cols], in_sem.at[c, j])
            for j, (src, dst) in enumerate(((k_hbm, k), (v_hbm, v), (g_hbm, g), (q_hbm, q)))
        ]

    for c in range(CHUNKS):
        for copy in loads(c):
            copy.start()

    barrier = pltpu.get_barrier_semaphore()
    everyone = (
        [(o, z * NY + p) for p in ypeers]
        + [(o, p * NY + y) for p in zpeers]
        + [(p, i) for p in opeers]
    )
    for peer in everyone:
        pl.semaphore_signal(barrier, inc=1, device_id=peer, device_id_type=MESH)

    offset = (o * (nz * NY) + i) * length
    rows = lax.broadcasted_iota(jnp.int32, (length, HEAD), 0) + offset
    scales = lax.rsqrt(rows.astype(F32) + 1.0)

    def send(src, dst, stage, c, peer):
        pltpu.make_async_remote_copy(
            src_ref=src, dst_ref=dst, send_sem=send_sem.at[stage, c], recv_sem=recv_sem.at[stage, c],
            device_id=peer, device_id_type=MESH,
        ).start()

    def arrived(ref, stage, c):
        pltpu.make_async_copy(ref, ref, recv_sem.at[stage, c]).wait()

    def states(c):
        for copy in loads(c):
            copy.wait()
        part = yrecv[c].shape[2]
        for j in range(PARTS[c]):
            cols = pl.ds((START[c] + j) * HEAD, HEAD)
            scaled = (g[:, cols].astype(F32) * scales).astype(BF16)
            sg[:, cols] = scaled
            both = (dot(k[:, cols], v[:, cols], TN), dot(q[:, cols], scaled, TN))
            for kind in range(2):
                for r in range(0, HEAD, part):
                    ysend[c][(j * HEAD + r) // part, kind] = both[kind][r:r + part].astype(BF16)
        if c == 0:
            pl.semaphore_wait(barrier, len(everyone))
        for p in ypeers:
            send(ysend[c].at[p], yrecv[c].at[y], 0, c, (o, z * NY + p))
        yrecv[c][y] = ysend[c][y]

    def group_sums(c):
        arrived(yrecv[c].at[pl.ds(0, NY - 1)], 0, c)
        total = yrecv[c][0].astype(F32)
        for p in range(1, NY):
            total = total + yrecv[c][p].astype(F32)
        sub = total.shape[1] // nz
        for p in range(nz):
            cut = slice(p * sub, (p + 1) * sub)
            zsend[c][p] = jnp.concatenate([total[0, cut], total[1, cut]], axis=0).astype(BF16)
        for p in zpeers:
            send(zsend[c].at[p], zrecv[c].at[z], 1, c, (o, p * NY + y))
        zrecv[c][z] = zsend[c][z]

    def outer_totals(c):
        arrived(zrecv[c].at[pl.ds(0, nz - 1)], 1, c)
        total = zrecv[c][0].astype(F32)
        for p in range(1, nz):
            total = total + zrecv[c][p].astype(F32)
        sub = total.shape[0] // 2
        tsend[c][0] = total[:sub]
        tsend[c][1] = total[sub:]
        for p in opeers:
            kind = jnp.where(p > o, 0, 1)
            send(tsend[c].at[kind], trecv[c].at[o], 2, c, (p, i))
        trecv[c][o] = jnp.zeros((sub, HEAD), F32)

    def offsets(c):
        arrived(trecv[c].at[pl.ds(0, no - 1)], 2, c)
        sub = trecv[c].shape[1]
        before = jnp.zeros((sub, HEAD), F32)
        after = jnp.zeros((sub, HEAD), F32)
        for p in range(no):
            part = trecv[c][p]
            before = before + jnp.where(p < o, part, 0.0)
            after = after + jnp.where(p > o, part, 0.0)
        own = [zrecv[c][p].astype(F32) for p in range(nz)]
        befores, afters = [], []
        for p in range(nz):
            befores.append(before)
            before = before + own[p][:sub]
        for p in reversed(range(nz)):
            afters.append(after)
            after = after + own[p][sub:]
        for p in range(nz):
            bsend[c][p] = jnp.concatenate([befores[p], afters[nz - 1 - p]], axis=0).astype(BF16)
        for p in zpeers:
            send(bsend[c].at[p], brecv[c].at[z], 3, c, (o, p * NY + y))
        brecv[c][z] = bsend[c][z]

    def block_states(c):
        arrived(brecv[c].at[pl.ds(0, nz - 1)], 3, c)
        sub = brecv[c].shape[1] // 2
        pieces = [brecv[c][p].astype(F32) for p in range(nz)]
        before = jnp.concatenate([piece[:sub] for piece in pieces], axis=0)
        after = jnp.concatenate([piece[sub:] for piece in pieces], axis=0)
        for r in range(NY):
            psend[c][r, 0] = before.astype(BF16)
            before = before + yrecv[c][r, 0].astype(F32)
        for r in reversed(range(NY)):
            psend[c][r, 1] = after.astype(BF16)
            after = after + yrecv[c][r, 1].astype(F32)
        for p in ypeers:
            send(psend[c].at[p], precv[c].at[y], 4, c, (o, z * NY + p))
        precv[c][y] = psend[c][y]

    def finish(c):
        arrived(precv[c].at[pl.ds(0, NY - 1)], 4, c)
        part = precv[c].shape[2]
        span = HEAD // part
        for j in range(PARTS[c]):
            cols = pl.ds((START[c] + j) * HEAD, HEAD)
            prefix, suffix = (
                jnp.concatenate([precv[c][j * span + r, kind] for r in range(span)], axis=0)
                for kind in range(2)
            )
            oq[:, cols] = (pq[:, cols] + dot(sg[:, cols], prefix, NT)).astype(BF16)
            ok[:, cols] = (pk[:, cols] + dot(v[:, cols], suffix, NT)).astype(BF16)
            ov[:, cols] = (pv[:, cols] + dot(k[:, cols], suffix, NN)).astype(BF16)

    def leave():
        cols = pl.ds(START[-1] * HEAD, PARTS[-1] * HEAD)
        for dst, src in ((lq, pq), (lk, pk), (lv, pv), (ls, sg), (lw, v), (lx, k)):
            dst[...] = src[:, cols]

    cut = length - HEAD

    def inside(head, carry):
        cols = pl.ds(pl.multiple_of(head * HEAD, HEAD), HEAD)
        kh, vh, qh, sh = k[:, cols], v[:, cols], q[:, cols], sg[:, cols]
        first = lax.broadcasted_iota(jnp.int32, (length, cut), 0)
        second = lax.broadcasted_iota(jnp.int32, (length, cut), 1)
        lower = second <= first
        upper = first <= second + HEAD
        row = lax.broadcasted_iota(jnp.int32, (HEAD, HEAD), 0)
        col = lax.broadcasted_iota(jnp.int32, (HEAD, HEAD), 1)

        def masked(a, b, mask):
            return jnp.where(mask, dot(a, b, NT), 0.0).astype(BF16)

        main = dot(masked(sh, vh[:cut], lower), kh[:cut], NN)
        rest = dot(masked(sh[cut:], vh[cut:], col <= row), kh[cut:], NN)
        pq[:cut, cols] = main[:cut]
        pq[cut:, cols] = main[cut:] + rest
        main = dot(masked(vh, sh[HEAD:], upper), qh[HEAD:], NN)
        rest = dot(masked(vh[:HEAD], sh[:HEAD], row <= col), qh[:HEAD], NN)
        pk[:HEAD, cols] = main[:HEAD] + rest
        pk[HEAD:, cols] = main[HEAD:]
        main = dot(masked(kh, qh[HEAD:], upper), sh[HEAD:], NN)
        rest = dot(masked(kh[:HEAD], qh[:HEAD], row <= col), sh[:HEAD], NN)
        pv[:HEAD, cols] = main[:HEAD] + rest
        pv[HEAD:, cols] = main[HEAD:]
        return carry

    actions = {
        "S": states, "R": group_sums, "T": outer_totals, "Z": offsets, "P": block_states, "F": finish,
    }
    for step in schedule():
        if step[0] == "I":
            lax.fori_loop(step[1], step[2], inside, 0)
        elif step[0] == "L":
            leave()
        else:
            actions[step[0]](step[1])

    arrived(last_states.at[pl.ds(0, NY - 1)], 4, CHUNKS - 1)
    for c in range(CHUNKS):
        for stage, (ref, count) in enumerate(
            ((ysend, NY), (zsend, nz), (trecv, no), (bsend, nz), (psend, NY))
        ):
            done = ref[c].at[pl.ds(0, count - 1)]
            pltpu.make_async_copy(done, done, send_sem.at[stage, c]).wait()


def outputs(oq, ok, ov, lq, lk, lv, ls, lw, lx, states, oq_hbm, ok_hbm, ov_hbm, fq, fk, fv, sem):
    early = pl.ds(0, START[-1] * HEAD)
    late = pl.ds(START[-1] * HEAD, PARTS[-1] * HEAD)
    copies = [
        pltpu.make_async_copy(src.at[:, early], dst.at[:, early], sem.at[0, j])
        for j, (src, dst) in enumerate(((oq, oq_hbm), (ok, ok_hbm), (ov, ov_hbm)))
    ]
    for copy in copies:
        copy.start()
    span = HEAD // states.shape[2]
    sides = [[], []]
    for j in range(PARTS[-1]):
        for kind in range(2):
            sides[kind].append(jnp.concatenate([states[j * span + r, kind] for r in range(span)], axis=0))
    plan = (
        (fq, lq, ls, sides[0], NT, oq_hbm), (fk, lk, lw, sides[1], NT, ok_hbm), (fv, lv, lx, sides[1], NN, ov_hbm)
    )
    for place, (full, part, left, side, dims, out) in enumerate(plan):
        for j in range(PARTS[-1]):
            cols = pl.ds(j * HEAD, HEAD)
            full[:, cols] = (part[:, cols] + dot(left[:, cols], side[j], dims)).astype(BF16)
        copy = pltpu.make_async_copy(full, out.at[:, late], sem.at[1, place])
        copy.start()
        copies.append(copy)
    for copy in copies:
        copy.wait()


def solution(mesh):
    no = mesh.shape["outer"]
    nz = mesh.shape["inner"] // NY

    def local(query_rows, key_rows, value_rows, grad_output):
        shape = query_rows.shape
        out = jax.ShapeDtypeStruct(shape, BF16)
        anywhere = pl.BlockSpec(memory_space=pltpu.HBM)
        inside = pl.BlockSpec(memory_space=pltpu.VMEM)
        rows = [heads * HEAD // NY for heads in PARTS]

        def buffers(make):
            return [make(count) for count in rows]

        wide = buffers(lambda count: pltpu.VMEM((NY, 2, count, HEAD), BF16))
        thin = buffers(lambda count: pltpu.VMEM((nz, 2 * (count // nz), HEAD), BF16))
        length, tail = shape[0], PARTS[-1] * HEAD
        narrow = jax.ShapeDtypeStruct((length, tail), BF16)
        sums = jax.ShapeDtypeStruct((length, tail), F32)
        last = jax.ShapeDtypeStruct((NY, 2, rows[-1], HEAD), BF16)
        held = pl.pallas_call(
            functools.partial(kernel, no, nz),
            name="linear_attention_grads",
            out_shape=(out,) * 3 + (sums,) * 3 + (narrow,) * 3 + (last,),
            in_specs=[anywhere] * 4,
            out_specs=(inside,) * 10,
            scratch_shapes=(
                [pltpu.VMEM(shape, BF16)] * 5
                + [pltpu.VMEM(shape, F32)] * 3
                + wide * 2
                + thin * 2
                + buffers(lambda count: pltpu.VMEM((2, count // nz, HEAD), F32))
                + buffers(lambda count: pltpu.VMEM((no, count // nz, HEAD), F32))
                + thin * 2
                + wide
                + wide[:-1]
                + [
                    pltpu.SemaphoreType.DMA((CHUNKS, 4)),
                    pltpu.SemaphoreType.DMA((5, CHUNKS)),
                    pltpu.SemaphoreType.DMA((5, CHUNKS)),
                ]
            ),
            compiler_params=pltpu.CompilerParams(
                collective_id=0, has_side_effects=True, vmem_limit_bytes=LIMIT
            ),
        )(query_rows, key_rows, value_rows, grad_output)
        return pl.pallas_call(
            outputs,
            name="write_grads",
            out_shape=(out, out, out),
            in_specs=[inside] * 10,
            out_specs=(anywhere,) * 3,
            scratch_shapes=[pltpu.VMEM((length, tail), BF16)] * 3 + [pltpu.SemaphoreType.DMA((2, 3))],
            compiler_params=pltpu.CompilerParams(vmem_limit_bytes=8 << 20),
        )(*held)

    placed = P(("outer", "inner"), None)
    return jax.shard_map(
        local, mesh=mesh, in_specs=(placed,) * 4, out_specs=(placed,) * 3, check_vma=False
    )
```

time: 47.8 us -> 45.3 us (0.948)
  local copies, waits for them, and re-layouts: 3.43 us -> 0 us
  Pallas kernels: 43.7 us -> 44.6 us
    unnamed x3 -> x0, local copies, waits for them, and re-layouts: 3.43 us -> none
    pallas_call x0 -> x1, Pallas kernels: none -> 2.24 us  [local(): pl.pallas_call(outputs, name='write_grads', out_shape=(out, out, out), in...]
    pallas_call x1, Pallas kernels: 43.7 us -> 42.4 us  [local(): pl.pallas_call(functools.partial(kernel, no, nz), name='linear_attention_...]
where the time goes in v2:
time: 45.3 us; the launch traced here: 45.2 us
  Pallas kernels  44.6 us (98%)
  between operations  0.64 us (1%)
    pallas_call x1, Pallas kernels, local(): pl.pallas_call(functools.partial(kernel, no, nz), name='linear_attention_...  42.4 us
    pallas_call x1, Pallas kernels, local(): pl.pallas_call(outputs, name='write_grads', out_shape=(out, out, out), in...  2.24 us

profile of v2, /device:TPU:1, one launch (start us, length us, event | category | flops | bytes accessed | tf_op | source)
XLA Modules:
  0.0 45.2 jit_solution(16282725597264703849)
XLA Ops:
  0.6 42.4 %linear_attention_grads.1 = (bf16[384,2048]{1,0:T(8,128)(2,1)S(1)}, bf16[384,2048]{1,0:T(8,128)(2,1)S(1)}, bf16[384,2048]{1,0:T(8,128)(2,1)S(1)}, f32[384,512]{1...) custom-call(bf16[384,2048]{1,0:T(8,128)(2,1)} %refs_0_.1, ...), custom_call_target="tpu_custom_call" | custom-call | tf_op jit(solution)/shard_map/linear_attention_grads/pallas_call | solution.py:312
  43.0 2.2 %write_grads.1 = (bf16[384,2048]{1,0:T(8,128)(2,1)}, bf16[384,2048]{1,0:T(8,128)(2,1)}, bf16[384,2048]{1,0:T(8,128)(2,1)}) custom-call(bf16[384,2048]{1,0:T(8,128)(2,1)S(1)} %get-tuple-element.13.oq, bf16[384,2048]{1,0:T(8,128)(2,1)S(1)} %get-tuple-element.14.ok, bf16[384,2048]{1,0:T(8,128)(2,1)S(1)} %get-tuple-element.15.ov, ...), custom_call_target="tpu_custom_call" | custom-call | tf_op jit(solution)/shard_map/write_grads/pallas_call | solution.py:338

commit v3 on v2

--- a/solution.py
+++ b/solution.py
@@ -14,14 +14,9 @@
 PARTS = (4, 4, 4, 4)
 CHUNKS = len(PARTS)
 ORDER = (
-    "S0 S1 S2 S3 "
-    "I6 R0 I2 R1 "
-    "I2 R2 T0 I2 "
-    "R3 T1 Z0 I2 "
-    "T2 Z1 I2 L0 "
-    "T3 P0 Z2 P1 "
-    "Z3 P2 P3 F0 "
-    "F1 F2 "
+    "S0", "S1", "S2", "S3", "I6", "R0", "I2", "R1", "I2", "R2", "T0", "I2",
+    "R3", "T1", "Z0", "I2", "T2", "Z1", "I2", "L0", "T3", "P0", "Z2", "P1",
+    "Z3", "P2", "P3", "F0", "F1", "F2",
 )
 LIMIT = 90 << 19
 START = [sum(PARTS[:c]) for c in range(CHUNKS)]
@@ -44,7 +39,7 @@
 def schedule():
     order = []
     inner = 0
-    for step in ORDER.split():
+    for step in ORDER:
         if step[0] == "I":
             count = int(step[1:])
             order.append(("I", inner, inner + count))

time: 45.3 us -> 45.3 us (level)
  no operation moved by 1% of the time
where the time goes in v3:
time: 45.3 us; the launch traced here: 45.2 us
  Pallas kernels  44.6 us (98%)
  between operations  0.64 us (1%)
    pallas_call x1, Pallas kernels, local(): pl.pallas_call(functools.partial(kernel, no, nz), name='linear_attention_...  42.4 us
    pallas_call x1, Pallas kernels, local(): pl.pallas_call(outputs, name='write_grads', out_shape=(out, out, out), in...  2.24 us

profile of v3, /device:TPU:1, one launch (start us, length us, event | category | flops | bytes accessed | tf_op | source)
XLA Modules:
  0.0 45.2 jit_solution(16282725597264703849)
XLA Ops:
  0.6 42.4 %linear_attention_grads.1 = (bf16[384,2048]{1,0:T(8,128)(2,1)S(1)}, bf16[384,2048]{1,0:T(8,128)(2,1)S(1)}, bf16[384,2048]{1,0:T(8,128)(2,1)S(1)}, f32[384,512]{1...) custom-call(bf16[384,2048]{1,0:T(8,128)(2,1)} %refs_0_.1, ...), custom_call_target="tpu_custom_call" | custom-call | tf_op jit(solution)/shard_map/linear_attention_grads/pallas_call | solution.py:307
  43.0 2.2 %write_grads.1 = (bf16[384,2048]{1,0:T(8,128)(2,1)}, bf16[384,2048]{1,0:T(8,128)(2,1)}, bf16[384,2048]{1,0:T(8,128)(2,1)}) custom-call(bf16[384,2048]{1,0:T(8,128)(2,1)S(1)} %get-tuple-element.13.oq, bf16[384,2048]{1,0:T(8,128)(2,1)S(1)} %get-tuple-element.14.ok, bf16[384,2048]{1,0:T(8,128)(2,1)S(1)} %get-tuple-element.15.ov, ...), custom_call_target="tpu_custom_call" | custom-call | tf_op jit(solution)/shard_map/write_grads/pallas_call | solution.py:333

commit v4 on v3

--- a/solution.py
+++ b/solution.py
@@ -11,12 +11,13 @@
 HEADS = 16
 HEAD = 128
 NY = 4
-PARTS = (4, 4, 4, 4)
+PARTS = (2, 2, 4, 4, 4)
 CHUNKS = len(PARTS)
 ORDER = (
-    "S0", "S1", "S2", "S3", "I6", "R0", "I2", "R1", "I2", "R2", "T0", "I2",
-    "R3", "T1", "Z0", "I2", "T2", "Z1", "I2", "L0", "T3", "P0", "Z2", "P1",
-    "Z3", "P2", "P3", "F0", "F1", "F2",
+    "S0", "S1", "S2", "S3", "S4", "I3", "R0", "R1", "I3", "R2", "I1", "T0",
+    "I1", "R3", "T1", "I1", "Z0", "R4", "T2", "Z1", "I1", "T3", "I1", "P0",
+    "Z2", "T4", "P1", "I1", "Z3", "I2", "P2", "Z4", "I2", "L0", "P3", "P4",
+    "F0", "F1", "F2", "F3",
 )
 LIMIT = 90 << 19
 START = [sum(PARTS[:c]) for c in range(CHUNKS)]
@@ -79,18 +80,20 @@
             for j, (src, dst) in enumerate(((k_hbm, k), (v_hbm, v), (g_hbm, g), (q_hbm, q)))
         ]
 
-    for c in range(CHUNKS):
-        for copy in loads(c):
-            copy.start()
+    for copy in loads(0):
+        copy.start()
 
     barrier = pltpu.get_barrier_semaphore()
     everyone = (
-        [(o, z * NY + p) for p in ypeers]
-        + [(o, p * NY + y) for p in zpeers]
+        [(o, p * NY + y) for p in zpeers]
         + [(p, i) for p in opeers]
+        + [(o, z * NY + p) for p in ypeers]
     )
     for peer in everyone:
         pl.semaphore_signal(barrier, inc=1, device_id=peer, device_id_type=MESH)
+    for c in range(1, CHUNKS):
+        for copy in loads(c):
+            copy.start()
 
     offset = (o * (nz * NY) + i) * length
     rows = lax.broadcasted_iota(jnp.int32, (length, HEAD), 0) + offset

time: 45.3 us -> 45.2 us (level)
  Pallas kernels: 44.6 us -> 44.1 us
    pallas_call x1, Pallas kernels: 42.4 us -> 41.9 us  [local(): pl.pallas_call(functools.partial(kernel, no, nz), name='linear_attention_...]
where the time goes in v4:
time: 45.2 us; the launch traced here: 44.9 us
  Pallas kernels  44.1 us (98%)
  between operations  0.8 us (2%)
    pallas_call x1, Pallas kernels, local(): pl.pallas_call(functools.partial(kernel, no, nz), name='linear_attention_...  41.9 us
    pallas_call x1, Pallas kernels, local(): pl.pallas_call(outputs, name='write_grads', out_shape=(out, out, out), in...  2.24 us

profile of v4, /device:TPU:1, one launch (start us, length us, event | category | flops | bytes accessed | tf_op | source)
XLA Modules:
  0.0 44.9 jit_solution(14375537520475356024)
XLA Ops:
  0.6 41.9 %linear_attention_grads.1 = (bf16[384,2048]{1,0:T(8,128)(2,1)S(1)}, bf16[384,2048]{1,0:T(8,128)(2,1)S(1)}, bf16[384,2048]{1,0:T(8,128)(2,1)S(1)}, f32[384,512]{1...) custom-call(bf16[384,2048]{1,0:T(8,128)(2,1)} %refs_0_.1, ...), custom_call_target="tpu_custom_call" | custom-call | tf_op jit(solution)/shard_map/linear_attention_grads/pallas_call | solution.py:310
  42.5 2.2 %write_grads.1 = (bf16[384,2048]{1,0:T(8,128)(2,1)}, bf16[384,2048]{1,0:T(8,128)(2,1)}, bf16[384,2048]{1,0:T(8,128)(2,1)}) custom-call(bf16[384,2048]{1,0:T(8,128)(2,1)S(1)} %get-tuple-element.13.oq, bf16[384,2048]{1,0:T(8,128)(2,1)S(1)} %get-tuple-element.14.ok, bf16[384,2048]{1,0:T(8,128)(2,1)S(1)} %get-tuple-element.15.ov, ...), custom_call_target="tpu_custom_call" | custom-call | tf_op jit(solution)/shard_map/write_grads/pallas_call | solution.py:336

commit v5 on v4

--- a/solution.py
+++ b/solution.py
@@ -14,10 +14,10 @@
 PARTS = (2, 2, 4, 4, 4)
 CHUNKS = len(PARTS)
 ORDER = (
-    "S0", "S1", "S2", "S3", "S4", "I3", "R0", "R1", "I3", "R2", "I1", "T0",
-    "I1", "R3", "T1", "I1", "Z0", "R4", "T2", "Z1", "I1", "T3", "I1", "P0",
-    "Z2", "T4", "P1", "I1", "Z3", "I2", "P2", "Z4", "I2", "L0", "P3", "P4",
-    "F0", "F1", "F2", "F3",
+    "S0", "S1", "S2", "S3", "S4", "I4", "R0", "R1", "I3", "R2", "I2", "R3",
+    "T0", "T1", "I1", "R4", "Z0", "T2", "Z1", "I2", "T3", "P0", "Z2", "T4",
+    "P1", "I1", "Z3", "P2", "I2", "Z4", "I1", "L0", "P3", "P4", "F0", "F1",
+    "F2", "F3",
 )
 LIMIT = 90 << 19
 START = [sum(PARTS[:c]) for c in range(CHUNKS)]

time: 45.2 us -> 47.5 us (1.051)
  Pallas kernels: 44.1 us -> 46.3 us
    pallas_call x1, Pallas kernels: 41.9 us -> 44.1 us  [local(): pl.pallas_call(functools.partial(kernel, no, nz), name='linear_attention_...]
where the time goes in v5:
time: 47.5 us; the launch traced here: 46.9 us
  Pallas kernels  46.3 us (97%)
  between operations  0.64 us (1%)
    pallas_call x1, Pallas kernels, local(): pl.pallas_call(functools.partial(kernel, no, nz), name='linear_attention_...  44.1 us
    pallas_call x1, Pallas kernels, local(): pl.pallas_call(outputs, name='write_grads', out_shape=(out, out, out), in...  2.24 us

profile of v5, /device:TPU:1, one launch (start us, length us, event | category | flops | bytes accessed | tf_op | source)
XLA Modules:
  0.0 46.9 jit_solution(5026346837508152113)
XLA Ops:
  0.6 44.1 %linear_attention_grads.1 = (bf16[384,2048]{1,0:T(8,128)(2,1)S(1)}, bf16[384,2048]{1,0:T(8,128)(2,1)S(1)}, bf16[384,2048]{1,0:T(8,128)(2,1)S(1)}, f32[384,512]{1...) custom-call(bf16[384,2048]{1,0:T(8,128)(2,1)} %refs_0_.1, ...), custom_call_target="tpu_custom_call" | custom-call | tf_op jit(solution)/shard_map/linear_attention_grads/pallas_call | solution.py:310
  44.7 2.2 %write_grads.1 = (bf16[384,2048]{1,0:T(8,128)(2,1)}, bf16[384,2048]{1,0:T(8,128)(2,1)}, bf16[384,2048]{1,0:T(8,128)(2,1)}) custom-call(bf16[384,2048]{1,0:T(8,128)(2,1)S(1)} %get-tuple-element.13.oq, bf16[384,2048]{1,0:T(8,128)(2,1)S(1)} %get-tuple-element.14.ok, bf16[384,2048]{1,0:T(8,128)(2,1)S(1)} %get-tuple-element.15.ov, ...), custom_call_target="tpu_custom_call" | custom-call | tf_op jit(solution)/shard_map/write_grads/pallas_call | solution.py:336
